TPU v7x, 256 devices: a whole 4x4x8 slice. The times are simulated.
256 devices in a mesh: tm: 16 (over z_lo, y, core), tile: 16 (over z_hi, x).
Axes of the slice: x: 4, y: 4, z: 8 (z_hi: 4, z_lo: 2; z = z_hi * 2 + z_lo), core: 2. Of those that a mesh axis runs over, the one named last changes fastest.
Arguments:
- queries: bfloat16 [65536, 4096], P(('tm', 'tile')), may hold values from -120 to 120
- keys: bfloat16 [65536, 4096], P(('tm', 'tile')), may hold values from -6 to 6
- values: bfloat16 [65536, 4096], P(('tm', 'tile')), may hold values from -6 to 6
- slot_tile: int32 [16, 16], replicated, may hold values from 0 to 15, each once within a row
- tile_mask: int32 [16, 16, 48], replicated, may hold values from 0 to 1, as said below
- token_count: int32 [16, 16], replicated, may hold values from 2 to 256
Outputs:
- attended: bfloat16 [65536, 4096], P(('tm', 'tile'))
Inputs may be any that keep to these rules, and one draw needn't show every extreme that they name: Each row of slot_tile holds every spatial tile of 0 .. 15 once. `tile_mask`: every row has at most 11 ones, and exactly 11 in some row of every slab; entry [s, t, 16 + t] is always 1; candidates in slab -1 or slab 16 are 0.
All inputs are finite; a program needn't handle non-finite values.
Results may differ from a plain program's by a relative error of at most 0.0049.
Values may be sent and summed in bfloat16 or wider, within the bound.
A program may use at most 128 MiB of HBM per device.

v0:
```python
import jax
import jax.numpy as jnp
from jax import lax
from jax.sharding import PartitionSpec as P

HEADS = 32
HEAD_DIM = 128
KMAX = 11
TILE_TOK = 256


def shifted(block, axis, distance):
    devices = range(lax.axis_size(axis))
    route = [(i - distance, i) for i in devices if i - distance in devices]
    return lax.ppermute(block, axis, route)


def tile_plan(slab_index, slot_tile, tile_mask, token_count):
    slab_count = slot_tile.shape[0]
    tile_count = slot_tile.shape[1]
    tile_order = jnp.arange(tile_count, dtype=jnp.int32)
    near_slabs = jnp.clip(slab_index + jnp.arange(3, dtype=jnp.int32) - 1, 0, slab_count - 1)
    near_slots = slot_tile[near_slabs]
    inverse = jnp.sum(
        jnp.where(
            near_slots[:, :, None] == tile_order[None, None, :], tile_order[None, :, None], 0
        ),
        axis=1,
    )
    own_spatial = slot_tile[slab_index]
    mask_rows = tile_mask[slab_index][own_spatial]
    picked = jnp.argsort(1 - mask_rows, axis=1, stable=True)[:, :KMAX]
    picked_flags = jnp.take_along_axis(mask_rows, picked, axis=1)
    cand_block = picked // tile_count
    cand_spatial = picked % tile_count
    key_block = cand_block * tile_count + inverse[cand_block, cand_spatial]
    near_counts = token_count[near_slabs]
    key_counts = near_counts[cand_block, cand_spatial]
    position = jnp.arange(TILE_TOK, dtype=jnp.int32)
    key_live = (picked_flags[:, :, None] > 0) & (position[None, None, :] < key_counts[:, :, None])
    query_live = position[None, :] < token_count[slab_index][own_spatial][:, None]
    return (key_block, key_live, query_live)


def head_major(rows, tile_count):
    local_heads = rows.shape[1]
    tiled = rows.reshape((tile_count, TILE_TOK, local_heads, HEAD_DIM))
    return jnp.transpose(tiled, (0, 2, 1, 3))


def tile_attention(query_tile, key_tiles, value_tiles, key_live, query_live):
    score_scale = 1.0 / HEAD_DIM**0.5
    scores = (
        jnp.einsum("hqd,khtd->hqkt", query_tile, key_tiles, preferred_element_type=jnp.float32)
        * score_scale
    )
    scores = jnp.where(key_live[None, None, :, :], scores, -1e30)
    row_max = jnp.max(scores, axis=(2, 3), keepdims=True)
    exponent = jnp.exp(scores - row_max)
    denominator = jnp.sum(exponent, axis=(2, 3), keepdims=True)
    weights = (exponent / denominator).astype(jnp.bfloat16)
    outputs = jnp.einsum("hqkt,khtd->hqd", weights, value_tiles, preferred_element_type=jnp.float32)
    outputs = jnp.where(query_live[None, :, None], outputs, 0.0)
    return outputs.astype(jnp.bfloat16)


def shards(queries, keys, values, slot_tile, tile_mask, token_count):
    tok_rows, feature_count = queries.shape
    head_shape = (tok_rows, HEADS, HEAD_DIM)
    query_heads = queries.reshape(head_shape)
    key_heads = keys.reshape(head_shape)
    value_heads = values.reshape(head_shape)
    earlier = shifted((key_heads, value_heads), "tm", 1)
    later_pair = shifted((key_heads, value_heads), "tm", -1)
    moved = (
        lax.all_to_all(query_heads, "tile", split_axis=1, concat_axis=0, tiled=True),
        lax.all_to_all(key_heads, "tile", split_axis=1, concat_axis=0, tiled=True),
        lax.all_to_all(value_heads, "tile", split_axis=1, concat_axis=0, tiled=True),
        lax.all_to_all(earlier[0], "tile", split_axis=1, concat_axis=0, tiled=True),
        lax.all_to_all(earlier[1], "tile", split_axis=1, concat_axis=0, tiled=True),
        lax.all_to_all(later_pair[0], "tile", split_axis=1, concat_axis=0, tiled=True),
        lax.all_to_all(later_pair[1], "tile", split_axis=1, concat_axis=0, tiled=True),
    )
    slab_queries, slab_keys, slab_values, keys_before, values_before, keys_after, values_after = (
        moved
    )
    local_heads = slab_queries.shape[1]
    tile_count = slot_tile.shape[1]
    near_keys = jnp.concatenate(
        [
            head_major(keys_before, tile_count),
            head_major(slab_keys, tile_count),
            head_major(keys_after, tile_count),
        ],
        0,
    )
    near_values = jnp.concatenate(
        [
            head_major(values_before, tile_count),
            head_major(slab_values, tile_count),
            head_major(values_after, tile_count),
        ],
        0,
    )
    query_tiles = head_major(slab_queries, tile_count)
    slab_index = lax.axis_index("tm")
    key_block, key_live, query_live = tile_plan(slab_index, slot_tile, tile_mask, token_count)

    def per_tile(tile_number):
        chosen = key_block[tile_number]
        return tile_attention(
            query_tiles[tile_number],
            near_keys[chosen],
            near_values[chosen],
            key_live[tile_number],
            query_live[tile_number],
        )

    attended = lax.map(per_tile, jnp.arange(tile_count, dtype=jnp.int32))
    attended = jnp.transpose(attended, (0, 2, 1, 3)).reshape(
        tile_count * TILE_TOK, local_heads, HEAD_DIM
    )
    restored = lax.all_to_all(attended, "tile", split_axis=0, concat_axis=1, tiled=True)
    return restored.reshape(tok_rows, feature_count)


def solution(mesh):
    in_specs = (
        P(("tm", "tile"), None),
        P(("tm", "tile"), None),
        P(("tm", "tile"), None),
        P(),
        P(),
        P(),
    )
    out_specs = P(("tm", "tile"), None)
    return jax.shard_map(shards, mesh=mesh, in_specs=in_specs, out_specs=out_specs, check_vma=False)
```

profile of v0, /device:TPU:27, one launch (start us, length us, event | category | flops | bytes accessed | tf_op | source)
XLA Modules:
  0.0 840.3 jit_solution(17858399752357740070)
XLA Ops:
  3.5 11.0 %all-to-all-start.2 = ((bf16[256,32,128]{2,0,1:T(8,128)(2,1)}), bf16[256,32,128]{2,0,1:T(8,128)(2,1)}, u32[]{:S(2)}, u32[]{:S(2)}) async-start(bf16[256,32,128]{2,0,1:T(8,128)(2,1)} %copy_bitcast_fusion.1), calls=%async_computation.2 | async-start | bytes 4194304 | tf_op jit(solution)/shard_map/all_to_all | solution.py:77
  16.5 45.0 %all-to-all-done.2 = bf16[256,32,128]{2,0,1:T(8,128)(2,1)} async-done(((bf16[256,32,128]{2,0,1:T(8,128)(2,1)}), bf16[256,32,128]{2,0,1:T(8,128)(2,1)}, u32[]{:S(2)}, u32[]{:S(2)}) %all-to-all-start.2) | async-done | bytes 2097184 | tf_op jit(solution)/shard_map/all_to_all | solution.py:77
  61.5 8.3 all-to-all-start.5
  74.8 84.6 %collective-permute-done = bf16[256,32,128]{2,0,1:T(8,128)(2,1)} collective-permute-done((bf16[256,32,128]{2,0,1:T(8,128)(2,1)S(1)}, bf16[256,32,128]{2,0,1:T(8,128)(2,1)}, u32[]{:S(2)}, u32[]{:S(2)}) %collective-permute-start) | collective-permute-done | bytes 2097184 | tf_op jit(solution)/shard_map/ppermute | solution.py:15
  159.4 8.8 %all-to-all-start.1 = ((bf16[256,32,128]{2,0,1:T(8,128)(2,1)}), bf16[256,32,128]{2,0,1:T(8,128)(2,1)}, u32[]{:S(2)}, u32[]{:S(2)}) async-start(bf16[256,32,128]{2,0,1:T(8,128)(2,1)} %collective-permute-done), calls=%async_computation.1 | async-start | bytes 4194304 | tf_op jit(solution)/shard_map/all_to_all | solution.py:79
  170.1 87.6 %collective-permute-done.1 = bf16[256,32,128]{2,0,1:T(8,128)(2,1)} collective-permute-done((bf16[256,32,128]{2,0,1:T(8,128)(2,1)S(1)}, bf16[256,32,128]{2,0,1:T(8,128)(2,1)}, u32[]{:S(2)}, u32[]{:S(2)}) %collective-permute-start.1) | collective-permute-done | bytes 2097184 | tf_op jit(solution)/shard_map/ppermute | solution.py:15
  257.7 8.9 %all-to-all-start.3 = ((bf16[256,32,128]{2,0,1:T(8,128)(2,1)}), bf16[256,32,128]{2,0,1:T(8,128)(2,1)S(1)}, u32[]{:S(2)}, u32[]{:S(2)}) async-start(bf16[256,32,128]{2,0,1:T(8,128)(2,1)} %collective-permute-done.1), calls=%async_computation.3 | async-start | bytes 4194304 | tf_op jit(solution)/shard_map/all_to_all | solution.py:81
  268.9 71.8 %collective-permute-done.2 = bf16[256,32,128]{2,0,1:T(8,128)(2,1)} collective-permute-done((bf16[256,32,128]{2,0,1:T(8,128)(2,1)}, bf16[256,32,128]{2,0,1:T(8,128)(2,1)}, u32[]{:S(2)}, u32[]{:S(2)}) %collective-permute-start.2) | collective-permute-done | bytes 2097184 | tf_op jit(solution)/shard_map/ppermute | solution.py:15
  341.9 8.9 %all-to-all-start.4 = ((bf16[256,32,128]{2,0,1:T(8,128)(2,1)}), bf16[256,32,128]{2,0,1:T(8,128)(2,1)}, u32[]{:S(2)}, u32[]{:S(2)}) async-start(bf16[256,32,128]{2,0,1:T(8,128)(2,1)} %collective-permute-done.2), calls=%async_computation.4 | async-start | bytes 4194304 | tf_op jit(solution)/shard_map/all_to_all | solution.py:80
  352.8 61.3 %collective-permute-done.3 = bf16[256,32,128]{2,0,1:T(8,128)(2,1)S(1)} collective-permute-done((bf16[256,32,128]{2,0,1:T(8,128)(2,1)}, bf16[256,32,128]{2,0,1:T(8,128)(2,1)S(1)}, u32[]{:S(2)}, u32[]{:S(2)}) %collective-permute-start.3) | collective-permute-done | bytes 2097184 | tf_op jit(solution)/shard_map/ppermute | solution.py:15
  415.4 8.8 %all-to-all-start.6 = ((bf16[256,32,128]{2,0,1:T(8,128)(2,1)}), bf16[256,32,128]{2,0,1:T(8,128)(2,1)S(1)}, u32[]{:S(2)}, u32[]{:S(2)}) async-start(bf16[256,32,128]{2,0,1:T(8,128)(2,1)} %copy-done.8), calls=%async_computation.6 | async-start | bytes 4194304 | tf_op jit(solution)/shard_map/all_to_all | solution.py:82
  427.6 19.1 %all-to-all-done.6 = bf16[256,32,128]{2,0,1:T(8,128)(2,1)S(1)} async-done(((bf16[256,32,128]{2,0,1:T(8,128)(2,1)}), bf16[256,32,128]{2,0,1:T(8,128)(2,1)S(1)}, u32[]{:S(2)}, u32[]{:S(2)}) %all-to-all-start.6) | async-done | bytes 2097184 | tf_op jit(solution)/shard_map/all_to_all | solution.py:82
  466.5 6.6 pad_maximum_fusion
  478.8 318.1 %while.10 = (s32[]{:T(128)}, bf16[16,2,256,128]{3,2,0,1:T(8,128)(2,1)}, s32[16]{0:T(128)S(1)}, pred[16,256]{1,0:T(8,128)(4,1)S(1)}, pred[16,11,256]{2,1,0:T(8,12...) while((s32[]{:T(128)}, ...), condition=%wide.region_5.6_spmd, body=%wide.region_2.5_spmd.sunk | while | flops 755630080 | bytes 49313196 | solution.py:119
  493.0 5.7 fusion.52
  512.8 5.7 fusion.52
  552.6 5.7 fusion.52
  572.5 5.7 fusion.52
  592.4 5.7 fusion.52
  632.1 5.7 fusion.52
  652.0 5.7 fusion.52
  671.9 5.7 fusion.52
  711.7 5.7 fusion.52
  801.7 31.5 %all_to_all.99 = bf16[4096,2,128]{2,1,0:T(2,128)(2,1)S(1)} all-to-all(bf16[4096,2,128]{2,1,0:T(2,128)(2,1)S(1)} %copy.92), channel_id=1, replica_groups=mesh['tm'=16,'tile'=16] {'tile'}, dimensions={0} | all-to-all | bytes 4194304 | tf_op jit(solution)/shard_map/all_to_all | solution.py:123
  (258 shorter events, 295.7 us)
Async XLA Ops:
  3.5 11.0 %copy-start.7 = (bf16[256,4096]{1,0:T(8,128)(2,1)S(1)}, bf16[256,4096]{1,0:T(8,128)(2,1)}, u32[]{:S(2)}) copy-start(bf16[256,4096]{1,0:T(8,128)(2,1)} %param.10) | copy-start | bytes 6291460
  3.5 58.0 %all-to-all-start.2 = ((bf16[256,32,128]{2,0,1:T(8,128)(2,1)}), bf16[256,32,128]{2,0,1:T(8,128)(2,1)}, u32[]{:S(2)}, u32[]{:S(2)}) async-start(bf16[256,32,128]{2,0,1:T(8,128)(2,1)} %copy_bitcast_fusion.1), calls=%async_computation.2 | async-start | bytes 4194304 | tf_op jit(solution)/shard_map/all_to_all | solution.py:77
  16.5 53.3 %copy-start.3 = (bf16[256,32,128]{2,0,1:T(8,128)(2,1)S(1)}, bf16[256,32,128]{2,0,1:T(8,128)(2,1)}, u32[]{:S(2)}) copy-start(bf16[256,32,128]{2,0,1:T(8,128)(2,1)} %copy_bitcast_fusion.1) | copy-start | bytes 6291460
  61.5 97.9 %all-to-all-start.5 = ((bf16[256,32,128]{2,0,1:T(8,128)(2,1)}), bf16[256,32,128]{2,0,1:T(8,128)(2,1)}, u32[]{:S(2)}, u32[]{:S(2)}) async-start(bf16[256,32,128]{2,0,1:T(8,128)(2,1)} %copy_bitcast_fusion), calls=%async_computation.5 | async-start | bytes 4194304 | tf_op jit(solution)/shard_map/all_to_all | solution.py:78
  69.7 89.6 %collective-permute-start = (bf16[256,32,128]{2,0,1:T(8,128)(2,1)S(1)}, bf16[256,32,128]{2,0,1:T(8,128)(2,1)}, u32[]{:S(2)}, u32[]{:S(2)}) collective-permute-start(bf16[256,32,128]{2,0,1:T(8,128)(2,1)S(1)} %copy-done.3), channel_id=1, source_target_pairs={{0,16},{16,32},{32,48},{48,64},{64,80},{80,96},{96,112},{112,128},... | collective-permute-start | bytes 6291464 | tf_op jit(solution)/shard_map/ppermute | solution.py:15
  159.4 98.4 %all-to-all-start.1 = ((bf16[256,32,128]{2,0,1:T(8,128)(2,1)}), bf16[256,32,128]{2,0,1:T(8,128)(2,1)}, u32[]{:S(2)}, u32[]{:S(2)}) async-start(bf16[256,32,128]{2,0,1:T(8,128)(2,1)} %collective-permute-done), calls=%async_computation.1 | async-start | bytes 4194304 | tf_op jit(solution)/shard_map/all_to_all | solution.py:79
  168.2 89.5 %collective-permute-start.1 = (bf16[256,32,128]{2,0,1:T(8,128)(2,1)S(1)}, bf16[256,32,128]{2,0,1:T(8,128)(2,1)}, u32[]{:S(2)}, u32[]{:S(2)}) collective-permute-start(bf16[256,32,128]{2,0,1:T(8,128)(2,1)S(1)} %copy-done.3), channel_id=1, source_target_pairs={{16,0},{32,16},{48,32},{64,48},{80,64},{96,80},{112,96},{128,112},... | collective-permute-start | bytes 6291464 | tf_op jit(solution)/shard_map/ppermute | solution.py:15
  257.7 82.9 %all-to-all-start.3 = ((bf16[256,32,128]{2,0,1:T(8,128)(2,1)}), bf16[256,32,128]{2,0,1:T(8,128)(2,1)S(1)}, u32[]{:S(2)}, u32[]{:S(2)}) async-start(bf16[256,32,128]{2,0,1:T(8,128)(2,1)} %collective-permute-done.1), calls=%async_computation.3 | async-start | bytes 4194304 | tf_op jit(solution)/shard_map/all_to_all | solution.py:81
  266.7 74.0 %collective-permute-start.2 = (bf16[256,32,128]{2,0,1:T(8,128)(2,1)}, bf16[256,32,128]{2,0,1:T(8,128)(2,1)}, u32[]{:S(2)}, u32[]{:S(2)}) collective-permute-start(bf16[256,32,128]{2,0,1:T(8,128)(2,1)} %copy_bitcast_fusion), channel_id=1, source_target_pairs={{0,16},{16,32},{32,48},{48,64},{64,80},{80,96},{96,112},{112,128},... | collective-permute-start | bytes 6291464 | tf_op jit(solution)/shard_map/ppermute | solution.py:15
  341.9 73.4 %all-to-all-start.4 = ((bf16[256,32,128]{2,0,1:T(8,128)(2,1)}), bf16[256,32,128]{2,0,1:T(8,128)(2,1)}, u32[]{:S(2)}, u32[]{:S(2)}) async-start(bf16[256,32,128]{2,0,1:T(8,128)(2,1)} %collective-permute-done.2), calls=%async_computation.4 | async-start | bytes 4194304 | tf_op jit(solution)/shard_map/all_to_all | solution.py:80
  350.9 63.2 %collective-permute-start.3 = (bf16[256,32,128]{2,0,1:T(8,128)(2,1)}, bf16[256,32,128]{2,0,1:T(8,128)(2,1)S(1)}, u32[]{:S(2)}, u32[]{:S(2)}) collective-permute-start(bf16[256,32,128]{2,0,1:T(8,128)(2,1)} %copy_bitcast_fusion), channel_id=1, source_target_pairs={{16,0},{32,16},{48,32},{64,48},{80,64},{96,80},{112,96},{128,112},... | collective-permute-start | bytes 6291464 | tf_op jit(solution)/shard_map/ppermute | solution.py:15
  415.4 31.3 %all-to-all-start.6 = ((bf16[256,32,128]{2,0,1:T(8,128)(2,1)}), bf16[256,32,128]{2,0,1:T(8,128)(2,1)S(1)}, u32[]{:S(2)}, u32[]{:S(2)}) async-start(bf16[256,32,128]{2,0,1:T(8,128)(2,1)} %copy-done.8), calls=%async_computation.6 | async-start | bytes 4194304 | tf_op jit(solution)/shard_map/all_to_all | solution.py:82
  427.6 25.6 %copy-start.9 = (s32[16,16]{1,0:T(8,128)S(1)}, s32[16,16]{1,0:T(8,128)}, u32[]{:S(2)}) copy-start(s32[16,16]{1,0:T(8,128)} %param.11) | copy-start | bytes 3076
  448.0 30.8 %all-to-all-start = ((bf16[256,32,128]{2,0,1:T(8,128)(2,1)}), bf16[256,32,128]{2,0,1:T(8,128)(2,1)}, u32[]{:S(2)}, u32[]{:S(2)}) async-start(bf16[256,32,128]{2,0,1:T(8,128)(2,1)} %copy_bitcast_fusion.2), calls=%async_computation | async-start | bytes 4194304 | tf_op jit(solution)/shard_map/all_to_all | solution.py:76
  455.8 3.3 copy-start.10
  466.5 6.6 copy-start.6
  486.8 2.5 copy-start.2
  506.7 2.5 copy-start.2
  526.6 2.5 copy-start.2
  546.5 2.5 copy-start.2
  566.4 2.5 copy-start.2
  586.3 2.5 copy-start.2
  665.8 2.5 copy-start.2
  836.1 4.2 copy-start.1
  (13 other events, 27.8 us)
where the time goes:
time: 852 us; the launch traced here: 840 us
  waiting for transfers between devices  369 us (43%)
  local copies, waits for them, and re-layouts  180 us (21%)
  matrix products  121 us (14%)
  starting transfers between devices  71 us (8%)
  other arithmetic  35.9 us (4%)
  blocking collectives  31.5 us (4%)
  loops' own time  30.8 us (4%)
    ppermute x4, waiting for transfers between devices, shifted(): return lax.ppermute(block, axis, route)  305 us
    dot_general x16, matrix products, tile_attention(): jnp.einsum('hqkt,khtd->hqd', weights, value_tiles, preferred_element_type...  91.5 us
    gather x16, local copies, waits for them, and re-layouts, per_tile(): near_keys[chosen]  57.7 us
    gather x16, local copies, waits for them, and re-layouts, per_tile(): near_values[chosen]  57.7 us
    all_to_all x1, waiting for transfers between devices, shards(): lax.all_to_all(key_heads, 'tile', split_axis=1, concat_axis=0, tiled=True)  45 us
    all_to_all x1, blocking collectives, shards(): lax.all_to_all(attended, 'tile', split_axis=0, concat_axis=1, tiled=True)  31.5 us
    another operation x1, loops' own time, shards(): attended = lax.map(per_tile, jnp.arange(tile_count, dtype=jnp.int32))  30.8 us
    dot_general x16, matrix products, tile_attention(): jnp.einsum('hqd,khtd->hqkt', query_tile, key_tiles, preferred_element_typ...  29.8 us
  transfers between devices with their start and end apart: 11, of which 6 were waited for; matrix products, arithmetic and copies ran while one was open for 4% of the time, Pallas kernels for 0%

commit v1 on v0

v1 whole, which is shorter than its diff:
```python
import functools

import jax
import jax.numpy as jnp
from jax import lax
from jax.experimental import pallas as pl
from jax.experimental.pallas import tpu as pltpu
from jax.sharding import PartitionSpec as P

HEAD_DIM = 128
KMAX = 11
SIDE = 4
EXP2_SCALE = 1.4426950408889634 / HEAD_DIM**0.5
MESH = pl.DeviceIdType.MESH


def peer(slot, step):
    row = (slot // SIDE + step + 1) % SIDE
    column = (slot % SIDE + step // SIDE + 1) % SIDE
    return row * SIDE + column


def kernel(
    slabs,
    tiles,
    slot_ref,
    mask_ref,
    count_ref,
    q_hbm,
    k_hbm,
    v_hbm,
    out_hbm,
    k0,
    k1,
    v0,
    v1,
    q0,
    q1,
    o0,
    o1,
    live,
    scores,
    follow,
    block_of,
    send_sem,
    recv_sem,
    own_sem,
    pass_sem,
    near_sem,
    out_send,
    out_recv,
    out_own,
):
    slab = lax.axis_index("tm")
    slot = lax.axis_index("tile")
    tok = q_hbm.shape[0]
    keys, values, query, result = (k0, k1), (v0, v1), (q0, q1), (o0, o1)
    has_before = slab > 0
    has_after = slab < slabs - 1
    near_count = has_before.astype(jnp.int32) + has_after.astype(jnp.int32)

    barrier = pltpu.get_barrier_semaphore()

    def greet(step, carry):
        pl.semaphore_signal(barrier, inc=1, device_id={"tile": peer(slot, step)}, device_id_type=MESH)
        return carry

    lax.fori_loop(0, tiles - 1, greet, 0)

    @pl.when(has_before)
    def _():
        pl.semaphore_signal(barrier, inc=1, device_id={"tm": slab - 1}, device_id_type=MESH)

    @pl.when(has_after)
    def _():
        pl.semaphore_signal(barrier, inc=1, device_id={"tm": slab + 1}, device_id_type=MESH)

    pl.semaphore_wait(barrier, tiles - 1 + near_count)

    phases = (
        (k_hbm, k0, tiles, 0),
        (v_hbm, v0, tiles, 0),
        (k_hbm, k1, tiles, 1),
        (v_hbm, v1, tiles, 1),
        (q_hbm, q0, 0, 0),
        (q_hbm, q1, 0, 1),
    )

    def head_columns(owner, head):
        return pl.ds(pl.multiple_of((owner * 2 + head) * HEAD_DIM, HEAD_DIM), HEAD_DIM)

    def own_copy(phase):
        source, gathered, base, head = phases[phase]
        return pltpu.make_async_copy(
            source.at[:, head_columns(slot, head)], gathered.at[base + slot], own_sem.at[phase]
        )

    def spread(phase):
        source, gathered, base, head = phases[phase]
        own_copy(phase).start()

        def send(step, carry):
            other = peer(slot, step)
            pltpu.make_async_remote_copy(
                src_ref=source.at[:, head_columns(other, head)],
                dst_ref=gathered.at[base + slot],
                send_sem=send_sem.at[phase],
                recv_sem=recv_sem.at[phase],
                device_id={"tile": other},
                device_id_type=MESH,
            ).start()
            return carry

        lax.fori_loop(0, tiles - 1, send, 0)

    def arrive(phase):
        gathered, base = phases[phase][1], phases[phase][2]
        others = gathered.at[pl.ds(base, tiles - 1)]
        pltpu.make_async_copy(others, others, recv_sem.at[phase]).wait()
        own_copy(phase).wait()

    def passing(phase, way):
        gathered = phases[phase][1]
        return pltpu.make_async_remote_copy(
            src_ref=gathered.at[pl.ds(tiles, tiles)],
            dst_ref=gathered.at[pl.ds(0 if way > 0 else 2 * tiles, tiles)],
            send_sem=pass_sem.at[phase, (1 + way) // 2],
            recv_sem=near_sem.at[phase, (1 + way) // 2],
            device_id={"tm": slab + way},
            device_id_type=MESH,
        )

    def hand_on(phase):
        @pl.when(has_after)
        def _():
            passing(phase, 1).start()

        @pl.when(has_before)
        def _():
            passing(phase, -1).start()

    def near_arrive(phase):
        @pl.when(has_before)
        def _():
            passing(phase, 1).wait_recv()

        @pl.when(has_after)
        def _():
            passing(phase, -1).wait_recv()

    spread(0)
    spread(1)

    row = lax.broadcasted_iota(jnp.int32, (tok, HEAD_DIM), 0)
    for block in range(3):
        near = jnp.clip(slab + (block - 1), 0, slabs - 1)

        def place(index, carry, near=near, block=block):
            found = jnp.int32(0)
            for other in range(tiles):
                found = jnp.where(slot_ref[near, other] == index, other, found)
            block_of[block * tiles + index] = block * tiles + found
            count = count_ref[near, slot_ref[near, index]]
            live[block * tiles + index] = jnp.where(row < count, 1.0, 0.0).astype(jnp.bfloat16)
            return carry

        lax.fori_loop(0, tiles, place, 0)
    live[3 * tiles] = jnp.zeros((tok, HEAD_DIM), jnp.bfloat16)

    def chain(tile, carry):
        follow[tile, 3 * tiles] = 3 * tiles
        follow[tile, 3 * tiles + 1] = 3 * tiles

        def link(index, after):
            candidate = 3 * tiles - 1 - index
            first = jnp.where(mask_ref[slab, tile, candidate] > 0, candidate, after)
            follow[tile, candidate] = first
            return first

        lax.fori_loop(0, 3 * tiles, link, jnp.int32(3 * tiles))
        return carry

    lax.fori_loop(0, tiles, chain, 0)

    for phase in range(4):
        arrive(phase)
        hand_on(phase)
        spread(phase + 2)

    def out_copy(head, other):
        return pltpu.make_async_remote_copy(
            src_ref=result[head].at[other],
            dst_ref=out_hbm.at[:, head_columns(slot, head)],
            send_sem=out_send.at[head],
            recv_sem=out_recv.at[head],
            device_id={"tile": other},
            device_id_type=MESH,
        )

    def out_keep(head):
        return pltpu.make_async_copy(
            result[head].at[slot], out_hbm.at[:, head_columns(slot, head)], out_own.at[head]
        )

    def attend(head, at):
        tile = slot_ref[slab, at]
        own_block = block_of[tiles + tile]
        chosen = []
        candidate = follow[tile, 0]
        for _ in range(KMAX):
            listed = candidate < 3 * tiles
            spot = block_of[jnp.minimum(candidate, 3 * tiles - 1)]
            chosen.append((jnp.where(listed, spot, own_block), jnp.where(listed, spot, 3 * tiles)))
            candidate = follow[tile, candidate + 1]
        q_tile = query[head][at]
        best = jnp.full((tok, HEAD_DIM), -jnp.inf, jnp.float32)
        for number, (spot, _) in enumerate(chosen):
            k_tile = keys[head][spot]
            alive = live[spot]
            k_tile = k_tile * alive + k_tile[0:1] * (1 - alive)
            score = lax.dot_general(
                q_tile, k_tile, (((1,), (1,)), ((), ())), preferred_element_type=jnp.float32
            )
            scores[number] = score
            for part in range(tok // HEAD_DIM):
                best = jnp.maximum(best, score[:, part * HEAD_DIM : (part + 1) * HEAD_DIM])
        top = jnp.max(best, axis=1, keepdims=True) * EXP2_SCALE
        total = jnp.zeros((tok, 2 * HEAD_DIM), jnp.float32)
        for number, (spot, life) in enumerate(chosen):
            alive = live[life]
            weight = jnp.exp2(scores[number] * EXP2_SCALE - top).astype(jnp.bfloat16)
            v_tile = jnp.concatenate([values[head][spot] * alive, alive], axis=1)
            total = total + jnp.dot(weight, v_tile, preferred_element_type=jnp.float32)
        attended = total[:, :HEAD_DIM] / total[:, HEAD_DIM:]
        count = count_ref[slab, tile]
        result[head][at] = jnp.where(row < count, attended, 0.0).astype(jnp.bfloat16)

    for head in range(2):
        near_arrive(2 * head)
        near_arrive(2 * head + 1)
        arrive(4 + head)

        def turn(step, carry, head=head):
            at = peer(slot, step)
            attend(head, at)

            @pl.when(at != slot)
            def _():
                out_copy(head, at).start()

            @pl.when(at == slot)
            def _():
                out_keep(head).start()

            return carry

        lax.fori_loop(0, tiles, turn, 0)

    for head in range(2):
        blocks = out_hbm.at[:, pl.ds(0, (tiles - 1) * HEAD_DIM)]
        pltpu.make_async_copy(blocks, blocks, out_recv.at[head]).wait()
        out_keep(head).wait()
        sent = result[head].at[pl.ds(0, tiles - 1)]
        pltpu.make_async_copy(sent, sent, out_send.at[head]).wait()
    for phase in range(6):
        sent = q0.at[pl.ds(0, tiles - 1)]
        pltpu.make_async_copy(sent, sent, send_sem.at[phase]).wait()
    for phase in range(4):

        @pl.when(has_after)
        def _(phase=phase):
            passing(phase, 1).wait_send()

        @pl.when(has_before)
        def _(phase=phase):
            passing(phase, -1).wait_send()


def solution(mesh):
    slabs, tiles = mesh.shape["tm"], mesh.shape["tile"]

    def shards(queries, keys, values, slot_tile, tile_mask, token_count):
        tok, width = queries.shape
        near = pltpu.VMEM((3 * tiles, tok, HEAD_DIM), jnp.bfloat16)
        own = pltpu.VMEM((tiles, tok, HEAD_DIM), jnp.bfloat16)
        return pl.pallas_call(
            functools.partial(kernel, slabs, tiles),
            out_shape=jax.ShapeDtypeStruct((tok, width), jnp.bfloat16),
            in_specs=[pl.BlockSpec(memory_space=pltpu.SMEM)] * 3
            + [pl.BlockSpec(memory_space=pl.ANY)] * 3,
            out_specs=pl.BlockSpec(memory_space=pl.ANY),
            scratch_shapes=[near] * 4
            + [own] * 4
            + [
                pltpu.VMEM((3 * tiles + 1, tok, HEAD_DIM), jnp.bfloat16),
                pltpu.VMEM((KMAX, tok, tok), jnp.float32),
                pltpu.SMEM((tiles, 3 * tiles + 2), jnp.int32),
                pltpu.SMEM((3 * tiles,), jnp.int32),
                pltpu.SemaphoreType.DMA((6,)),
                pltpu.SemaphoreType.DMA((6,)),
                pltpu.SemaphoreType.DMA((6,)),
                pltpu.SemaphoreType.DMA((4, 2)),
                pltpu.SemaphoreType.DMA((4, 2)),
                pltpu.SemaphoreType.DMA((2,)),
                pltpu.SemaphoreType.DMA((2,)),
                pltpu.SemaphoreType.DMA((2,)),
            ],
            compiler_params=pltpu.CompilerParams(
                collective_id=0, has_side_effects=True, vmem_limit_bytes=48 * 1024 * 1024
            ),
        )(slot_tile, tile_mask, token_count, queries, keys, values)

    return jax.shard_map(
        shards,
        mesh=mesh,
        in_specs=(P(("tm", "tile"), None),) * 3 + (P(),) * 3,
        out_specs=P(("tm", "tile"), None),
        check_vma=False,
    )
```

time: 852 us -> 268 us (0.31); the launches traced: 840 us -> 268 us
  waiting for transfers between devices: 369 us -> 0 us
  Pallas kernels: 0 us -> 263 us
  local copies, waits for them, and re-layouts: 180 us -> 5.21 us
  matrix products: 121 us -> 0 us
  starting transfers between devices: 71 us -> 0 us
  other arithmetic: 35.9 us -> 0 us
  blocking collectives: 31.5 us -> 0 us
  loops' own time: 30.8 us -> 0 us
    ppermute x4 -> x0, waiting for transfers between devices: 305 us -> none  [shifted(): return lax.ppermute(block, axis, route)]
    pallas_call x0 -> x1, Pallas kernels: none -> 263 us  [shards(): pl.pallas_call(functools.partial(kernel, slabs, tiles), out_shape=jax.Sha...]
    gather x46 -> x0, local copies, waits for them, and re-layouts: 126 us -> none  [the longest x16 57.7 us: per_tile(): near_keys[chosen]]
    dot_general x32 -> x0, matrix products: 121 us -> none  [the longest x16 91.5 us: tile_attention(): jnp.einsum('hqkt,khtd->hqd', weights, value_tiles, preferred_element_type...]
    all_to_all x7 -> x0, waiting for transfers between devices: 64.1 us -> none  [the longest x1 45 us: shards(): lax.all_to_all(key_heads, 'tile', split_axis=1, concat_axis=0, tiled=True)]
    all_to_all x7 -> x0, starting transfers between devices: 59.9 us -> none  [the longest x1 11 us: shards(): lax.all_to_all(key_heads, 'tile', split_axis=1, concat_axis=0, tiled=True)]
    all_to_all x1 -> x0, blocking collectives: 31.5 us -> none  [shards(): lax.all_to_all(attended, 'tile', split_axis=0, concat_axis=1, tiled=True)]
    another operation x1 -> x0, loops' own time: 30.8 us -> none  [shards(): attended = lax.map(per_tile, jnp.arange(tile_count, dtype=jnp.int32))]
  transfers between devices with their start and end apart: 11 -> 0, of which waited for: 6 -> 0; matrix products, arithmetic and copies ran while one was open for 4% -> 0% of each run, Pallas kernels for 0% -> 0%
where the time goes in v1:
time: 268 us
  Pallas kernels  263 us (98%)
  local copies, waits for them, and re-layouts  5.21 us (2%)
    pallas_call x1, Pallas kernels, shards(): pl.pallas_call(functools.partial(kernel, slabs, tiles), out_shape=jax.Sha...  263 us

profile of v1, /device:TPU:27, one launch (start us, length us, event | category | flops | bytes accessed | tf_op | source)
XLA Modules:
  0.0 268.2 jit_solution(3708261038010800098)
XLA Ops:
  0.0 0.0 copy-start
  0.0 1.6 copy-done
  1.6 0.0 copy-start.1
  1.6 0.9 copy-done.1
  2.5 0.0 copy-start.2
  2.5 0.7 copy-done.2
  3.2 0.0 copy-start.3
  3.2 0.7 copy-done.3
  3.9 263.0 %shard_map.64 = bf16[256,4096]{1,0:T(8,128)(2,1)S(1)} custom-call(s32[16,16]{1,0:T(8,128)S(1)} %copy-done.2, s32[16,16,48]{2,1,0:T(8,128)S(1)} %copy-done.1, s32[16,16]{1,0:T(8,128)S(1)} %copy-done.3, bf16[256,4096]{1,0:T(8,128)(2,1)S(1)} %copy-done, bf16[256,4096]{1,0:T(8,128)(2,1)} %k_hbm.1, bf16[256,4096]{1,0:T(8,128)(2,1)} %v_hbm.1), custom_call_target="tpu_custom_call" | custom-call | tf_op jit(solution)/shard_map/pallas_call | solution.py:286
  266.9 1.3 copy.8
Async XLA Ops:
  0.0 1.6 copy-start
  1.6 0.9 copy-start.1
  2.5 0.7 copy-start.2
  3.2 0.7 copy-start.3

commit v2 on v1

v2 whole, which is shorter than its diff:
```python
import functools

import jax
import jax.numpy as jnp
from jax import lax
from jax.experimental import pallas as pl
from jax.experimental.pallas import tpu as pltpu
from jax.sharding import PartitionSpec as P

HEAD_DIM = 128
KMAX = 11
SIDE = 4
AHEAD = 2
VMEM_BYTES = 60 * 1024 * 1024
EXP2_SCALE = 1.4426950408889634 / HEAD_DIM**0.5
MESH = pl.DeviceIdType.MESH


def peer(slot, step):
    row = (slot // SIDE + step + 1) % SIDE
    column = (slot % SIDE + step // SIDE + 1) % SIDE
    return row * SIDE + column


def origin(slot, step):
    row = (slot // SIDE + 5 * SIDE - 1 - step) % SIDE
    column = (slot % SIDE + 2 * SIDE - 1 - step // SIDE) % SIDE
    return row * SIDE + column


def kernel(
    slabs,
    tiles,
    slot_hbm,
    mask_hbm,
    count_hbm,
    q_hbm,
    k_hbm,
    v_hbm,
    out_hbm,
    k0,
    k1,
    v0,
    v1,
    q0,
    q1,
    o0,
    o1,
    live,
    score0,
    score1,
    top0,
    top1,
    k_raw,
    v_raw,
    fixed,
    relay,
    slot_ref,
    mask_ref,
    count_ref,
    follow,
    block_of,
    key_pick,
    value_pick,
    plan_sem,
    send_sem,
    recv_sem,
    query_sem,
    own_sem,
    pass_sem,
    near_sem,
    relay_send,
    relay_sem,
    out_send,
    out_recv,
    out_own,
):
    slab = lax.axis_index("tm")
    slot = lax.axis_index("tile")
    tok = q_hbm.shape[0]
    keys, values, query, result = (k0, k1), (v0, v1), (q0, q1), (o0, o1)
    has_before = slab > 0
    has_after = slab < slabs - 1
    near_count = has_before.astype(jnp.int32) + has_after.astype(jnp.int32)

    right = slabs // 2
    left = right - 1
    via_left = (left - 2, left - 4, left - 6)
    via_right = tuple(slabs - 1 - other for other in via_left)
    part = tiles // (len(via_left) + 1)
    at_meeting = (slab == left) | (slab == right)
    is_via = slab == via_left[0]
    for other in via_left[1:] + via_right:
        is_via = is_via | (slab == other)

    plan = [
        pltpu.make_async_copy(slot_hbm, slot_ref, plan_sem.at[0]),
        pltpu.make_async_copy(mask_hbm.at[slab], mask_ref, plan_sem.at[1]),
        pltpu.make_async_copy(count_hbm, count_ref, plan_sem.at[2]),
    ]
    raw = [
        pltpu.make_async_copy(k_hbm, k_raw, plan_sem.at[3]),
        pltpu.make_async_copy(v_hbm, v_raw, plan_sem.at[4]),
    ]
    for copy in plan + raw:
        copy.start()

    barrier = pltpu.get_barrier_semaphore()

    def greet_slab(other):
        pl.semaphore_signal(barrier, inc=1, device_id={"tm": other}, device_id_type=MESH)

    def greet(step, carry):
        pl.semaphore_signal(barrier, inc=1, device_id={"tile": peer(slot, step)}, device_id_type=MESH)
        return carry

    lax.fori_loop(0, tiles - 1, greet, 0)

    @pl.when(has_before)
    def _():
        greet_slab(slab - 1)

    @pl.when(has_after)
    def _():
        greet_slab(slab + 1)

    @pl.when(at_meeting)
    def _():
        for other in via_left + via_right:
            greet_slab(other)

    @pl.when(is_via)
    def _():
        greet_slab(left)
        greet_slab(right)

    extra = 6 * at_meeting.astype(jnp.int32) + 2 * is_via.astype(jnp.int32)
    pl.semaphore_wait(barrier, tiles - 1 + near_count + extra)

    for copy in plan + raw:
        copy.wait()
    row = lax.broadcasted_iota(jnp.int32, (tok, HEAD_DIM), 0)
    own_count = count_ref[slab, slot_ref[slab, slot]]
    own_alive = jnp.where(row < own_count, 1.0, 0.0).astype(jnp.bfloat16)

    phases = (
        (k_raw, k0, tiles, 0),
        (v_raw, v0, tiles, 0),
        (k_raw, k1, tiles, 1),
        (v_raw, v1, tiles, 1),
        (q_hbm, q0, 0, 0),
        (q_hbm, q1, 0, 1),
    )

    def head_columns(owner, head):
        return pl.ds(pl.multiple_of((owner * 2 + head) * HEAD_DIM, HEAD_DIM), HEAD_DIM)

    def own_query(head):
        return pltpu.make_async_copy(
            q_hbm.at[:, head_columns(slot, head)], query[head].at[slot], own_sem.at[head]
        )

    def spread(phase):
        source, gathered, base, head = phases[phase]
        if phase >= 4:
            own_query(head).start()

        def send(step, carry):
            other = peer(slot, step)
            if phase < 4:
                block = source[:, head_columns(other, head)]
                if phase % 2 == 0:
                    block = block * own_alive + block[0:1] * (1 - own_alive)
                else:
                    block = block * own_alive
                fixed[phase, other] = block
            pltpu.make_async_remote_copy(
                src_ref=fixed.at[phase, other] if phase < 4 else source.at[:, head_columns(other, head)],
                dst_ref=gathered.at[base + slot],
                send_sem=send_sem.at[phase],
                recv_sem=recv_sem.at[phase] if phase < 4 else query_sem.at[head, slot],
                device_id={"tile": other},
                device_id_type=MESH,
            ).start()
            return carry

        lax.fori_loop(0, tiles - 1, send, 0)
        if phase < 4:
            block = source[:, head_columns(slot, head)]
            if phase % 2 == 0:
                block = block * own_alive + block[0:1] * (1 - own_alive)
            else:
                block = block * own_alive
            gathered[base + slot] = block

    def arrive(phase):
        gathered, base = phases[phase][1], phases[phase][2]
        others = gathered.at[pl.ds(base, tiles - 1)]
        pltpu.make_async_copy(others, others, recv_sem.at[phase]).wait()

    def passing(phase, way, first=0, blocks=None):
        gathered = phases[phase][1]
        blocks = tiles if blocks is None else blocks
        return pltpu.make_async_remote_copy(
            src_ref=gathered.at[pl.ds(tiles + first, blocks)],
            dst_ref=gathered.at[pl.ds((0 if way > 0 else 2 * tiles) + first, blocks)],
            send_sem=pass_sem.at[phase, (1 + way) // 2],
            recv_sem=near_sem.at[phase, (1 + way) // 2],
            device_id={"tm": slab + way},
            device_id_type=MESH,
        )

    def to_relay(phase, index, other):
        return pltpu.make_async_remote_copy(
            src_ref=phases[phase][1].at[pl.ds(tiles + (index + 1) * part, part)],
            dst_ref=relay.at[phase],
            send_sem=relay_send.at[phase, index],
            recv_sem=relay_sem.at[phase],
            device_id={"tm": other},
            device_id_type=MESH,
        )

    def from_relay(phase, index, way):
        first = (0 if way > 0 else 2 * tiles) + (index + 1) * part
        return pltpu.make_async_remote_copy(
            src_ref=relay.at[phase],
            dst_ref=phases[phase][1].at[pl.ds(first, part)],
            send_sem=relay_send.at[phase, index],
            recv_sem=near_sem.at[phase, (1 + way) // 2],
            device_id={"tm": right if way > 0 else left},
            device_id_type=MESH,
        )

    def hand_on(phase):
        @pl.when(has_after & (slab != left))
        def _():
            passing(phase, 1).start()

        @pl.when(has_before & (slab != right))
        def _():
            passing(phase, -1).start()

        @pl.when(slab == left)
        def _():
            for index, other in enumerate(via_left):
                to_relay(phase, index, other).start()
            passing(phase, 1, 0, part).start()

        @pl.when(slab == right)
        def _():
            for index, other in enumerate(via_right):
                to_relay(phase, index, other).start()
            passing(phase, -1, 0, part).start()

    def relay_on(phase):
        for way, vias in ((1, via_left), (-1, via_right)):
            for index, other in enumerate(vias):

                @pl.when(slab == other)
                def _(way=way, index=index):
                    pltpu.make_async_copy(relay.at[phase], relay.at[phase], relay_sem.at[phase]).wait()
                    from_relay(phase, index, way).start()

    def near_arrive(phase):
        @pl.when(has_before)
        def _():
            passing(phase, 1).wait_recv()

        @pl.when(has_after)
        def _():
            passing(phase, -1).wait_recv()

    def handed_on(phase):
        @pl.when(has_after & (slab != left))
        def _():
            passing(phase, 1).wait_send()

        @pl.when(has_before & (slab != right))
        def _():
            passing(phase, -1).wait_send()

        for way, here, vias in ((1, left, via_left), (-1, right, via_right)):

            @pl.when(slab == here)
            def _(way=way, vias=vias):
                passing(phase, way, 0, part).wait_send()
                for index, other in enumerate(vias):
                    to_relay(phase, index, other).wait_send()

            for index, other in enumerate(vias):

                @pl.when(slab == other)
                def _(way=way, index=index):
                    from_relay(phase, index, way).wait_send()

    for phase in range(AHEAD):
        spread(phase)

    for block in range(3):
        near = jnp.clip(slab + (block - 1), 0, slabs - 1)

        def place(index, carry, near=near, block=block):
            found = jnp.int32(0)
            for other in range(tiles):
                found = jnp.where(slot_ref[near, other] == index, other, found)
            block_of[block * tiles + index] = block * tiles + found
            count = count_ref[near, slot_ref[near, index]]
            live[block * tiles + index] = jnp.where(row < count, 1.0, 0.0).astype(jnp.bfloat16)
            return carry

        lax.fori_loop(0, tiles, place, 0)
    nothing = jnp.zeros((tok, HEAD_DIM), jnp.bfloat16)
    live[3 * tiles] = nothing
    v0[3 * tiles] = nothing
    v1[3 * tiles] = nothing

    def chain(tile, carry):
        follow[tile, 3 * tiles] = 3 * tiles
        follow[tile, 3 * tiles + 1] = 3 * tiles

        def link(index, after):
            candidate = 3 * tiles - 1 - index
            first = jnp.where(mask_ref[tile, candidate] > 0, candidate, after)
            follow[tile, candidate] = first
            return first

        lax.fori_loop(0, 3 * tiles, link, jnp.int32(3 * tiles))
        return carry

    lax.fori_loop(0, tiles, chain, 0)

    def pick(at, carry):
        tile = slot_ref[slab, at]
        own_block = block_of[tiles + tile]
        candidate = follow[tile, 0]
        for number in range(KMAX):
            listed = candidate < 3 * tiles
            spot = block_of[jnp.minimum(candidate, 3 * tiles - 1)]
            key_pick[at, number] = jnp.where(listed, spot, own_block)
            value_pick[at, number] = jnp.where(listed, spot, 3 * tiles)
            candidate = follow[tile, candidate + 1]
        return carry

    lax.fori_loop(0, tiles, pick, 0)

    for phase in range(4):
        arrive(phase)
        hand_on(phase)
        if phase > 0:
            relay_on(phase - 1)
        if phase + AHEAD < len(phases):
            spread(phase + AHEAD)
    relay_on(3)

    def out_copy(head, other):
        return pltpu.make_async_remote_copy(
            src_ref=result[head].at[other],
            dst_ref=out_hbm.at[:, head_columns(slot, head)],
            send_sem=out_send.at[head],
            recv_sem=out_recv.at[head],
            device_id={"tile": other},
            device_id_type=MESH,
        )

    def out_keep(head):
        return pltpu.make_async_copy(
            result[head].at[slot], out_hbm.at[:, head_columns(slot, head)], out_own.at[head]
        )

    def work(head, ahead, ahead_scores, ahead_top, at=None, at_scores=None, at_top=None):
        q_tile = query[head][ahead]
        best = jnp.full((tok, HEAD_DIM), -jnp.inf, jnp.float32)
        if at is not None:
            top = jnp.concatenate([at_top[...]] * (tok // HEAD_DIM), axis=1)
            total = jnp.zeros((tok, 2 * HEAD_DIM), jnp.float32)
        for number in range(KMAX):
            score = lax.dot_general(
                q_tile,
                keys[head][key_pick[ahead, number]],
                (((1,), (1,)), ((), ())),
                preferred_element_type=jnp.float32,
            )
            ahead_scores[number] = score
            if at is not None:
                weight = jnp.exp2(at_scores[number] * EXP2_SCALE - top).astype(jnp.bfloat16)
                spot = value_pick[at, number]
                v_tile = jnp.concatenate([values[head][spot], live[spot]], axis=1)
                total = total + jnp.dot(weight, v_tile, preferred_element_type=jnp.float32)
            for start in range(0, tok, HEAD_DIM):
                best = jnp.maximum(best, score[:, start : start + HEAD_DIM])
        ahead_top[...] = jnp.broadcast_to(
            jnp.max(best, axis=1, keepdims=True) * EXP2_SCALE, (tok, HEAD_DIM)
        )
        if at is not None:
            attended = total[:, :HEAD_DIM] / total[:, HEAD_DIM:]
            count = count_ref[slab, slot_ref[slab, at]]
            result[head][at] = jnp.where(row < count, attended, 0.0).astype(jnp.bfloat16)

    def query_arrive(head, step):
        at = origin(slot, step)

        @pl.when(step < tiles - 1)
        def _():
            block = query[head].at[at]
            pltpu.make_async_copy(block, block, query_sem.at[head, at]).wait()

        @pl.when(step == tiles - 1)
        def _():
            own_query(head).wait()

    for head in range(2):
        near_arrive(2 * head)
        near_arrive(2 * head + 1)
        query_arrive(head, 0)
        work(head, origin(slot, 0), score0, top0)

        def turn(pair, carry, head=head):
            even = 2 * pair
            query_arrive(head, even + 1)
            work(head, origin(slot, even + 1), score1, top1, origin(slot, even), score0, top0)
            out_copy(head, origin(slot, even)).start()

            @pl.when(even + 2 < tiles)
            def _():
                query_arrive(head, even + 2)

            later = jnp.minimum(even + 2, tiles - 1)
            work(head, origin(slot, later), score0, top0, origin(slot, even + 1), score1, top1)

            @pl.when(even + 2 < tiles)
            def _():
                out_copy(head, origin(slot, even + 1)).start()

            @pl.when(even + 2 == tiles)
            def _():
                out_keep(head).start()

            return carry

        lax.fori_loop(0, tiles // 2, turn, 0)

    for head in range(2):
        blocks = out_hbm.at[:, pl.ds(0, (tiles - 1) * HEAD_DIM)]
        pltpu.make_async_copy(blocks, blocks, out_recv.at[head]).wait()
        out_keep(head).wait()
        gone = result[head].at[pl.ds(0, tiles - 1)]
        pltpu.make_async_copy(gone, gone, out_send.at[head]).wait()
    for phase in range(6):
        gone = q0.at[pl.ds(0, tiles - 1)]
        pltpu.make_async_copy(gone, gone, send_sem.at[phase]).wait()
    for phase in range(4):
        handed_on(phase)


def solution(mesh):
    slabs, tiles = mesh.shape["tm"], mesh.shape["tile"]

    def shards(queries, keys, values, slot_tile, tile_mask, token_count):
        tok, width = queries.shape
        near = pltpu.VMEM((3 * tiles, tok, HEAD_DIM), jnp.bfloat16)
        near_zero = pltpu.VMEM((3 * tiles + 1, tok, HEAD_DIM), jnp.bfloat16)
        own = pltpu.VMEM((tiles, tok, HEAD_DIM), jnp.bfloat16)
        return pl.pallas_call(
            functools.partial(kernel, slabs, tiles),
            out_shape=jax.ShapeDtypeStruct((tok, width), jnp.bfloat16),
            in_specs=[pl.BlockSpec(memory_space=pl.ANY)] * 6,
            out_specs=pl.BlockSpec(memory_space=pl.ANY),
            scratch_shapes=[near, near, near_zero, near_zero]
            + [own] * 4
            + [
                near_zero,
                pltpu.VMEM((KMAX, tok, tok), jnp.float32),
                pltpu.VMEM((KMAX, tok, tok), jnp.float32),
                pltpu.VMEM((tok, HEAD_DIM), jnp.float32),
                pltpu.VMEM((tok, HEAD_DIM), jnp.float32),
                pltpu.VMEM((tok, width), jnp.bfloat16),
                pltpu.VMEM((tok, width), jnp.bfloat16),
                pltpu.VMEM((4, tiles, tok, HEAD_DIM), jnp.bfloat16),
                pltpu.VMEM((4, tiles // 4, tok, HEAD_DIM), jnp.bfloat16),
                pltpu.SMEM(slot_tile.shape, jnp.int32),
                pltpu.SMEM(tile_mask.shape[1:], jnp.int32),
                pltpu.SMEM(token_count.shape, jnp.int32),
                pltpu.SMEM((tiles, 3 * tiles + 2), jnp.int32),
                pltpu.SMEM((3 * tiles,), jnp.int32),
                pltpu.SMEM((tiles, KMAX), jnp.int32),
                pltpu.SMEM((tiles, KMAX), jnp.int32),
                pltpu.SemaphoreType.DMA((5,)),
                pltpu.SemaphoreType.DMA((6,)),
                pltpu.SemaphoreType.DMA((4,)),
                pltpu.SemaphoreType.DMA((2, tiles)),
                pltpu.SemaphoreType.DMA((2,)),
                pltpu.SemaphoreType.DMA((4, 2)),
                pltpu.SemaphoreType.DMA((4, 2)),
                pltpu.SemaphoreType.DMA((4, 3)),
                pltpu.SemaphoreType.DMA((4,)),
                pltpu.SemaphoreType.DMA((2,)),
                pltpu.SemaphoreType.DMA((2,)),
                pltpu.SemaphoreType.DMA((2,)),
            ],
            compiler_params=pltpu.CompilerParams(
                collective_id=0, has_side_effects=True, vmem_limit_bytes=VMEM_BYTES
            ),
        )(slot_tile, tile_mask, token_count, queries, keys, values)

    return jax.shard_map(
        shards,
        mesh=mesh,
        in_specs=(P(("tm", "tile"), None),) * 3 + (P(),) * 3,
        out_specs=P(("tm", "tile"), None),
        check_vma=False,
    )
```

time: 268 us -> 209 us (0.78)
  Pallas kernels: 263 us -> 204 us
    pallas_call x1, Pallas kernels: 263 us -> 204 us  [shards(): pl.pallas_call(functools.partial(kernel, slabs, tiles), out_shape=jax.Sha...]
where the time goes in v2:
time: 209 us; the launch traced here: 207 us
  Pallas kernels  204 us (98%)
  local copies, waits for them, and re-layouts  3.13 us (1%)
    pallas_call x1, Pallas kernels, shards(): pl.pallas_call(functools.partial(kernel, slabs, tiles), out_shape=jax.Sha...  204 us

profile of v2, /device:TPU:27, one launch (start us, length us, event | category | flops | bytes accessed | tf_op | source)
XLA Modules:
  0.0 207.5 jit_solution(15244563641348998599)
XLA Ops:
  0.0 204.3 %shard_map.64 = bf16[256,4096]{1,0:T(8,128)(2,1)} custom-call(s32[16,16]{1,0:T(8,128)} %slot_hbm.1, s32[16,16,48]{2,1,0:T(8,128)} %mask_hbm.1, s32[16,16]{1,0:T(8,128)} %count_hbm.1, bf16[256,4096]{1,0:T(8,128)(2,1)} %q_hbm.1, bf16[256,4096]{1,0:T(8,128)(2,1)} %k_hbm.1, bf16[256,4096]{1,0:T(8,128)(2,1)} %v_hbm.1), custom_call_target="tpu_custom_call" | custom-call | tf_op jit(solution)/shard_map/pallas_call | solution.py:463
  204.3 3.1 %copy.8 = bf16[256,4096]{1,0:T(8,128)(2,1)} copy(bf16[256,4096]{1,0:T(8,128)(2,1)} %shard_map.64) | data formatting | bytes 4194304

commit v3 on v0

v3 whole, which is shorter than its diff:
```python
import functools

import jax
import jax.numpy as jnp
from jax import lax
from jax.experimental import pallas as pl
from jax.experimental.pallas import tpu as pltpu
from jax.sharding import PartitionSpec as P

HEAD_DIM = 128
KMAX = 11
SIDE = 4
RING = 8
OWNERS = SIDE * RING
VMEM_BYTES = 60 * 1024 * 1024
EXP2_SCALE = 1.4426950408889634 / HEAD_DIM**0.5
MESH = pl.DeviceIdType.MESH


def kernel(
    slabs,
    tiles,
    slot_hbm,
    mask_hbm,
    count_hbm,
    q_hbm,
    k_hbm,
    v_hbm,
    out_hbm,
    keys,
    values,
    query,
    result,
    live,
    score0,
    score1,
    top0,
    top1,
    k_raw,
    v_raw,
    k_fixed,
    v_fixed,
    slot_ref,
    mask_ref,
    count_ref,
    follow,
    block_of,
    key_pick,
    value_pick,
    plan_sem,
    send_sem,
    recv_sem,
    query_sem,
    own_sem,
    pass_sem,
    near_sem,
    out_send,
    out_recv,
    out_own,
):
    half_slabs = slabs // 2
    near = 3 * tiles
    slab = lax.axis_index("tm")
    slot = lax.axis_index("tile")
    half, place = slab // half_slabs, slab % half_slabs
    z, x = 2 * (slot // SIDE) + half, slot % SIDE
    tok = q_hbm.shape[0]

    def device(other_z, other_x):
        other_slab = (other_z % 2) * half_slabs + place
        return {"tm": other_slab, "tile": (other_z // 2) * SIDE + other_x}

    def partner(step):
        return (z + step + 1) % RING, (x + step // RING + 1) % SIDE

    def origin(step):
        return (z + 5 * RING - 1 - step) % RING, (x + 2 * SIDE - 1 - step // RING) % SIDE

    def block_at(other_z, other_x):
        return (other_z % 2) * tiles + (other_z // 2) * SIDE + other_x

    def head_columns(other_z, other_x):
        return pl.ds(pl.multiple_of((other_z * SIDE + other_x) * HEAD_DIM, HEAD_DIM), HEAD_DIM)

    first = [
        pltpu.make_async_copy(slot_hbm, slot_ref, plan_sem.at[0]),
        pltpu.make_async_copy(mask_hbm.at[place], mask_ref.at[0], plan_sem.at[1]),
        pltpu.make_async_copy(mask_hbm.at[place + half_slabs], mask_ref.at[1], plan_sem.at[2]),
        pltpu.make_async_copy(count_hbm, count_ref, plan_sem.at[3]),
        pltpu.make_async_copy(k_hbm, k_raw, plan_sem.at[4]),
        pltpu.make_async_copy(v_hbm, v_raw, plan_sem.at[5]),
    ]
    for copy in first:
        copy.start()

    def beside(way):
        return {"tm": half * half_slabs + (place + half_slabs + way) % half_slabs}

    barrier = pltpu.get_barrier_semaphore()

    def greet(step, carry):
        pl.semaphore_signal(
            barrier, inc=1, device_id=device(*partner(step)), device_id_type=MESH
        )
        return carry

    lax.fori_loop(0, OWNERS - 1, greet, 0)
    for way in (1, -1):
        pl.semaphore_signal(barrier, inc=1, device_id=beside(way), device_id_type=MESH)
    pl.semaphore_wait(barrier, OWNERS + 1)

    for copy in first:
        copy.wait()
    row = lax.broadcasted_iota(jnp.int32, (tok, HEAD_DIM), 0)
    own_count = count_ref[slab, slot_ref[slab, slot]]
    own_alive = jnp.where(row < own_count, 1.0, 0.0).astype(jnp.bfloat16)
    own_block = half * near + tiles + slot

    def k_block(columns):
        block = k_raw[:, columns]
        return block * own_alive + block[0:1] * (1 - own_alive)

    def v_block(columns):
        return v_raw[:, columns] * own_alive

    def own_query():
        return pltpu.make_async_copy(
            q_hbm.at[:, head_columns(z, x)], query.at[block_at(z, x)], own_sem.at[0]
        )

    spans = ((0, OWNERS // 2), (OWNERS // 2, OWNERS - 1))

    def spread(part):
        kind = part // 2
        start, stop = spans[part % 2]

        def send(step, carry):
            other = partner(step)
            columns = head_columns(*other)
            if kind == 0:
                k_fixed[step] = k_block(columns)
                source, target, arrived = k_fixed.at[step], keys.at[own_block], recv_sem.at[part]
            elif kind == 1:
                v_fixed[step] = v_block(columns)
                source, target, arrived = v_fixed.at[step], values.at[own_block], recv_sem.at[part]
            else:
                source, target = q_hbm.at[:, columns], query.at[block_at(z, x)]
                arrived = query_sem.at[block_at(z, x)]
            pltpu.make_async_remote_copy(
                src_ref=source,
                dst_ref=target,
                send_sem=send_sem.at[part],
                recv_sem=arrived,
                device_id=device(*other),
                device_id_type=MESH,
            ).start()
            return carry

        lax.fori_loop(start, stop, send, 0)
        if part == 1:
            keys[own_block] = k_block(head_columns(z, x))
        elif part == 3:
            values[own_block] = v_block(head_columns(z, x))
        elif part == 5:
            own_query().start()

    def arrive(part):
        start, stop = spans[part % 2]
        blocks = (keys, values)[part // 2].at[pl.ds(0, stop - start)]
        pltpu.make_async_copy(blocks, blocks, recv_sem.at[part]).wait()

    def passing(kind, way, which):
        gathered = (keys, values)[kind]
        turned = place == (half_slabs - 1 if way > 0 else 0)
        target = which + way * turned.astype(jnp.int32)
        exists = (target >= 0) & (target < 2)
        target = jnp.clip(target, 0, 1)
        copy = pltpu.make_async_remote_copy(
            src_ref=gathered.at[pl.ds(which * near + tiles, tiles)],
            dst_ref=gathered.at[pl.ds(target * near + (0 if way > 0 else 2 * tiles), tiles)],
            send_sem=pass_sem.at[kind, (1 + way) // 2, which],
            recv_sem=near_sem.at[kind, (1 + way) // 2, target],
            device_id=beside(way),
            device_id_type=MESH,
        )
        return exists, copy

    def hand_on(kind):
        for way in (1, -1):
            for which in range(2):
                exists, copy = passing(kind, way, which)
                pl.when(exists)(copy.start)

    def handed_on(kind):
        for way in (1, -1):
            for which in range(2):
                exists, copy = passing(kind, way, which)
                pl.when(exists)(copy.wait_send)

    def near_arrive(kind):
        for way in (1, -1):
            for which in range(2):
                before = place + half_slabs * which - way
                blocks = (keys, values)[kind].at[pl.ds(0, tiles)]
                copy = pltpu.make_async_copy(
                    blocks, blocks, near_sem.at[kind, (1 + way) // 2, which]
                )
                pl.when((before >= 0) & (before < slabs))(copy.wait)

    spread(0)
    spread(1)

    nothing = jnp.zeros((tok, HEAD_DIM), jnp.bfloat16)
    live[2 * near] = nothing
    values[2 * near] = nothing
    for which in range(2):
        for block in range(3):
            there = jnp.clip(place + half_slabs * which + (block - 1), 0, slabs - 1)
            base = which * near + block * tiles

            def seat(index, carry, there=there, base=base):
                found = jnp.int32(0)
                for other in range(tiles):
                    found = jnp.where(slot_ref[there, other] == index, other, found)
                block_of[base + index] = base + found
                count = count_ref[there, slot_ref[there, index]]
                live[base + index] = jnp.where(row < count, 1.0, 0.0).astype(jnp.bfloat16)
                return carry

            lax.fori_loop(0, tiles, seat, 0)

        def chain(tile, carry, which=which):
            at = which * tiles + tile
            follow[at, near] = near
            follow[at, near + 1] = near

            def link(index, after):
                candidate = near - 1 - index
                listed = jnp.where(mask_ref[which, tile, candidate] > 0, candidate, after)
                follow[at, candidate] = listed
                return listed

            lax.fori_loop(0, near, link, jnp.int32(near))
            return carry

        lax.fori_loop(0, tiles, chain, 0)

        def pick(at, carry, which=which):
            tile = slot_ref[place + half_slabs * which, at]
            centre = block_of[which * near + tiles + tile]
            candidate = follow[which * tiles + tile, 0]
            for number in range(KMAX):
                listed = candidate < near
                spot = block_of[which * near + jnp.minimum(candidate, near - 1)]
                key_pick[which * tiles + at, number] = jnp.where(listed, spot, centre)
                value_pick[which * tiles + at, number] = jnp.where(listed, spot, 2 * near)
                candidate = follow[which * tiles + tile, candidate + 1]
            return carry

        lax.fori_loop(0, tiles, pick, 0)

    for part in range(4):
        arrive(part)
        if part % 2 == 1:
            hand_on(part // 2)
        spread(part + 2)

    def out_copy(step):
        other = origin(step)
        return pltpu.make_async_remote_copy(
            src_ref=result.at[block_at(*other)],
            dst_ref=out_hbm.at[:, head_columns(z, x)],
            send_sem=out_send.at[0],
            recv_sem=out_recv.at[0],
            device_id=device(*other),
            device_id_type=MESH,
        )

    def out_keep():
        return pltpu.make_async_copy(
            result.at[block_at(z, x)], out_hbm.at[:, head_columns(z, x)], out_own.at[0]
        )

    def work(ahead, ahead_scores, ahead_top, at=None, at_scores=None, at_top=None):
        q_tile = query[ahead]
        best = jnp.full((tok, HEAD_DIM), -jnp.inf, jnp.float32)
        if at is not None:
            top = jnp.concatenate([at_top[...]] * (tok // HEAD_DIM), axis=1)
            total = jnp.zeros((tok, 2 * HEAD_DIM), jnp.float32)
        for number in range(KMAX):
            score = lax.dot_general(
                q_tile,
                keys[key_pick[ahead, number]],
                (((1,), (1,)), ((), ())),
                preferred_element_type=jnp.float32,
            )
            ahead_scores[number] = score
            if at is not None:
                weight = jnp.exp2(at_scores[number] * EXP2_SCALE - top).astype(jnp.bfloat16)
                spot = value_pick[at, number]
                v_tile = jnp.concatenate([values[spot], live[spot]], axis=1)
                total = total + jnp.dot(weight, v_tile, preferred_element_type=jnp.float32)
            for start in range(0, tok, HEAD_DIM):
                best = jnp.maximum(best, score[:, start : start + HEAD_DIM])
        ahead_top[...] = jnp.broadcast_to(
            jnp.max(best, axis=1, keepdims=True) * EXP2_SCALE, (tok, HEAD_DIM)
        )
        if at is not None:
            attended = total[:, :HEAD_DIM] / total[:, HEAD_DIM:]
            at_half, at_slot = at // tiles, at % tiles
            at_slab = place + half_slabs * at_half
            count = count_ref[at_slab, slot_ref[at_slab, at_slot]]
            result[at] = jnp.where(row < count, attended, 0.0).astype(jnp.bfloat16)

    def query_arrive(step):
        at = block_at(*origin(step))

        @pl.when(step < OWNERS - 1)
        def _():
            block = query.at[at]
            pltpu.make_async_copy(block, block, query_sem.at[at]).wait()

        @pl.when(step == OWNERS - 1)
        def _():
            own_query().wait()

    near_arrive(0)
    near_arrive(1)
    query_arrive(0)
    work(block_at(*origin(0)), score0, top0)

    def turn(pair, carry):
        even = 2 * pair
        at, after = block_at(*origin(even)), block_at(*origin(even + 1))
        query_arrive(even + 1)
        work(after, score1, top1, at, score0, top0)
        out_copy(even).start()

        @pl.when(even + 2 < OWNERS)
        def _():
            query_arrive(even + 2)

        later = block_at(*origin(jnp.minimum(even + 2, OWNERS - 1)))
        work(later, score0, top0, after, score1, top1)

        @pl.when(even + 2 < OWNERS)
        def _():
            out_copy(even + 1).start()

        @pl.when(even + 2 == OWNERS)
        def _():
            out_keep().start()

        return carry

    lax.fori_loop(0, OWNERS // 2, turn, 0)

    blocks = out_hbm.at[:, pl.ds(0, (OWNERS - 1) * HEAD_DIM)]
    pltpu.make_async_copy(blocks, blocks, out_recv.at[0]).wait()
    out_keep().wait()
    gone = result.at[pl.ds(0, OWNERS - 1)]
    pltpu.make_async_copy(gone, gone, out_send.at[0]).wait()
    for part in range(6):
        start, stop = spans[part % 2]
        gone = query.at[pl.ds(0, stop - start)]
        pltpu.make_async_copy(gone, gone, send_sem.at[part]).wait()
    handed_on(0)
    handed_on(1)


def solution(mesh):
    slabs, tiles = mesh.shape["tm"], mesh.shape["tile"]

    def shards(queries, keys, values, slot_tile, tile_mask, token_count):
        tok, width = queries.shape
        near = 3 * tiles

        def blocks(number):
            return pltpu.VMEM((number, tok, HEAD_DIM), jnp.bfloat16)

        return pl.pallas_call(
            functools.partial(kernel, slabs, tiles),
            out_shape=jax.ShapeDtypeStruct((tok, width), jnp.bfloat16),
            in_specs=[pl.BlockSpec(memory_space=pl.ANY)] * 6,
            out_specs=pl.BlockSpec(memory_space=pl.ANY),
            scratch_shapes=[
                blocks(2 * near),
                blocks(2 * near + 1),
                blocks(2 * tiles),
                blocks(2 * tiles),
                blocks(2 * near + 1),
                pltpu.VMEM((KMAX, tok, tok), jnp.float32),
                pltpu.VMEM((KMAX, tok, tok), jnp.float32),
                pltpu.VMEM((tok, HEAD_DIM), jnp.float32),
                pltpu.VMEM((tok, HEAD_DIM), jnp.float32),
                pltpu.VMEM((tok, width), jnp.bfloat16),
                pltpu.VMEM((tok, width), jnp.bfloat16),
                blocks(OWNERS),
                blocks(OWNERS),
                pltpu.SMEM(slot_tile.shape, jnp.int32),
                pltpu.SMEM((2,) + tile_mask.shape[1:], jnp.int32),
                pltpu.SMEM(token_count.shape, jnp.int32),
                pltpu.SMEM((2 * tiles, near + 2), jnp.int32),
                pltpu.SMEM((2 * near,), jnp.int32),
                pltpu.SMEM((2 * tiles, KMAX), jnp.int32),
                pltpu.SMEM((2 * tiles, KMAX), jnp.int32),
                pltpu.SemaphoreType.DMA((6,)),
                pltpu.SemaphoreType.DMA((6,)),
                pltpu.SemaphoreType.DMA((4,)),
                pltpu.SemaphoreType.DMA((2 * tiles,)),
                pltpu.SemaphoreType.DMA((1,)),
                pltpu.SemaphoreType.DMA((2, 2, 2)),
                pltpu.SemaphoreType.DMA((2, 2, 2)),
                pltpu.SemaphoreType.DMA((1,)),
                pltpu.SemaphoreType.DMA((1,)),
                pltpu.SemaphoreType.DMA((1,)),
            ],
            compiler_params=pltpu.CompilerParams(
                collective_id=0, has_side_effects=True, vmem_limit_bytes=VMEM_BYTES
            ),
        )(slot_tile, tile_mask, token_count, queries, keys, values)

    return jax.shard_map(
        shards,
        mesh=mesh,
        in_specs=(P(("tm", "tile"), None),) * 3 + (P(),) * 3,
        out_specs=P(("tm", "tile"), None),
        check_vma=False,
    )
```

time: 852 us -> 195 us (0.23); the launches traced: 840 us -> 193 us
  waiting for transfers between devices: 369 us -> 0 us
  Pallas kernels: 0 us -> 190 us
  local copies, waits for them, and re-layouts: 180 us -> 3.13 us
  matrix products: 121 us -> 0 us
  starting transfers between devices: 71 us -> 0 us
  other arithmetic: 35.9 us -> 0 us
  blocking collectives: 31.5 us -> 0 us
  loops' own time: 30.8 us -> 0 us
    ppermute x4 -> x0, waiting for transfers between devices: 305 us -> none  [shifted(): return lax.ppermute(block, axis, route)]
    pallas_call x0 -> x1, Pallas kernels: none -> 190 us  [shards(): pl.pallas_call(functools.partial(kernel, slabs, tiles), out_shape=jax.Sha...]
    gather x46 -> x0, local copies, waits for them, and re-layouts: 126 us -> none  [the longest x16 57.7 us: per_tile(): near_keys[chosen]]
    dot_general x32 -> x0, matrix products: 121 us -> none  [the longest x16 91.5 us: tile_attention(): jnp.einsum('hqkt,khtd->hqd', weights, value_tiles, preferred_element_type...]
    all_to_all x7 -> x0, waiting for transfers between devices: 64.1 us -> none  [the longest x1 45 us: shards(): lax.all_to_all(key_heads, 'tile', split_axis=1, concat_axis=0, tiled=True)]
    all_to_all x7 -> x0, starting transfers between devices: 59.9 us -> none  [the longest x1 11 us: shards(): lax.all_to_all(key_heads, 'tile', split_axis=1, concat_axis=0, tiled=True)]
    all_to_all x1 -> x0, blocking collectives: 31.5 us -> none  [shards(): lax.all_to_all(attended, 'tile', split_axis=0, concat_axis=1, tiled=True)]
    another operation x1 -> x0, loops' own time: 30.8 us -> none  [shards(): attended = lax.map(per_tile, jnp.arange(tile_count, dtype=jnp.int32))]
  transfers between devices with their start and end apart: 11 -> 0, of which waited for: 6 -> 0; matrix products, arithmetic and copies ran while one was open for 4% -> 0% of each run, Pallas kernels for 0% -> 0%
where the time goes in v3:
time: 195 us; the launch traced here: 193 us
  Pallas kernels  190 us (97%)
  local copies, waits for them, and re-layouts  3.13 us (2%)
    pallas_call x1, Pallas kernels, shards(): pl.pallas_call(functools.partial(kernel, slabs, tiles), out_shape=jax.Sha...  190 us

profile of v3, /device:TPU:27, one launch (start us, length us, event | category | flops | bytes accessed | tf_op | source)
XLA Modules:
  0.0 193.2 jit_solution(7291507564388343109)
XLA Ops:
  0.0 190.0 %shard_map.64 = bf16[256,4096]{1,0:T(8,128)(2,1)} custom-call(s32[16,16]{1,0:T(8,128)} %slot_hbm.1, s32[16,16,48]{2,1,0:T(8,128)} %mask_hbm.1, s32[16,16]{1,0:T(8,128)} %count_hbm.1, bf16[256,4096]{1,0:T(8,128)(2,1)} %q_hbm.1, bf16[256,4096]{1,0:T(8,128)(2,1)} %k_hbm.1, bf16[256,4096]{1,0:T(8,128)(2,1)} %v_hbm.1), custom_call_target="tpu_custom_call" | custom-call | tf_op jit(solution)/shard_map/pallas_call | solution.py:381
  190.0 3.1 %copy.8 = bf16[256,4096]{1,0:T(8,128)(2,1)} copy(bf16[256,4096]{1,0:T(8,128)(2,1)} %shard_map.64) | data formatting | bytes 4194304

commit v4 on v3

--- a/solution.py
+++ b/solution.py
@@ -12,7 +12,8 @@
 SIDE = 4
 RING = 8
 OWNERS = SIDE * RING
-VMEM_BYTES = 60 * 1024 * 1024
+SETTLE_PARTS = 4
+VMEM_BYTES = 56 * 1024 * 1024
 EXP2_SCALE = 1.4426950408889634 / HEAD_DIM**0.5
 MESH = pl.DeviceIdType.MESH
 
@@ -82,17 +83,16 @@
     def head_columns(other_z, other_x):
         return pl.ds(pl.multiple_of((other_z * SIDE + other_x) * HEAD_DIM, HEAD_DIM), HEAD_DIM)
 
+    upper, lower = pl.ds(0, tok // 2), pl.ds(tok // 2, tok // 2)
     first = [
         pltpu.make_async_copy(slot_hbm, slot_ref, plan_sem.at[0]),
-        pltpu.make_async_copy(mask_hbm.at[place], mask_ref.at[0], plan_sem.at[1]),
-        pltpu.make_async_copy(mask_hbm.at[place + half_slabs], mask_ref.at[1], plan_sem.at[2]),
-        pltpu.make_async_copy(count_hbm, count_ref, plan_sem.at[3]),
-        pltpu.make_async_copy(k_hbm, k_raw, plan_sem.at[4]),
-        pltpu.make_async_copy(v_hbm, v_raw, plan_sem.at[5]),
+        pltpu.make_async_copy(count_hbm, count_ref, plan_sem.at[1]),
+        pltpu.make_async_copy(k_hbm.at[upper], k_raw.at[upper], plan_sem.at[2]),
+        pltpu.make_async_copy(k_hbm.at[lower], k_raw.at[lower], plan_sem.at[3]),
+        pltpu.make_async_copy(v_hbm, v_raw, plan_sem.at[4]),
+        pltpu.make_async_copy(mask_hbm.at[place], mask_ref.at[0], plan_sem.at[5]),
+        pltpu.make_async_copy(mask_hbm.at[place + half_slabs], mask_ref.at[1], plan_sem.at[6]),
     ]
-    for copy in first:
-        copy.start()
-
     def beside(way):
         return {"tm": half * half_slabs + (place + half_slabs + way) % half_slabs}
 
@@ -107,9 +107,11 @@
     lax.fori_loop(0, OWNERS - 1, greet, 0)
     for way in (1, -1):
         pl.semaphore_signal(barrier, inc=1, device_id=beside(way), device_id_type=MESH)
+    for copy in first:
+        copy.start()
     pl.semaphore_wait(barrier, OWNERS + 1)
 
-    for copy in first:
+    for copy in first[:4]:
         copy.wait()
     row = lax.broadcasted_iota(jnp.int32, (tok, HEAD_DIM), 0)
     own_count = count_ref[slab, slot_ref[slab, slot]]
@@ -209,6 +211,8 @@
 
     spread(0)
     spread(1)
+    for copy in first[4:]:
+        copy.wait()
 
     nothing = jnp.zeros((tok, HEAD_DIM), jnp.bfloat16)
     live[2 * near] = nothing
@@ -368,6 +372,20 @@
     handed_on(1)
 
 
+def settle(source, target, held, sems):
+    rows = source.shape[0] // SETTLE_PARTS
+    spans = [pl.ds(part * rows, rows) for part in range(SETTLE_PARTS)]
+    come = [pltpu.make_async_copy(source.at[s], held.at[s], sems.at[0, i]) for i, s in enumerate(spans)]
+    go = [pltpu.make_async_copy(held.at[s], target.at[s], sems.at[1, i]) for i, s in enumerate(spans)]
+    for copy in come:
+        copy.start()
+    for before, after in zip(come, go):
+        before.wait()
+        after.start()
+    for copy in go:
+        copy.wait()
+
+
 def solution(mesh):
     slabs, tiles = mesh.shape["tm"], mesh.shape["tile"]
 
@@ -378,7 +396,7 @@
         def blocks(number):
             return pltpu.VMEM((number, tok, HEAD_DIM), jnp.bfloat16)
 
-        return pl.pallas_call(
+        attended = pl.pallas_call(
             functools.partial(kernel, slabs, tiles),
             out_shape=jax.ShapeDtypeStruct((tok, width), jnp.bfloat16),
             in_specs=[pl.BlockSpec(memory_space=pl.ANY)] * 6,
@@ -404,7 +422,7 @@
                 pltpu.SMEM((2 * near,), jnp.int32),
                 pltpu.SMEM((2 * tiles, KMAX), jnp.int32),
                 pltpu.SMEM((2 * tiles, KMAX), jnp.int32),
-                pltpu.SemaphoreType.DMA((6,)),
+                pltpu.SemaphoreType.DMA((7,)),
                 pltpu.SemaphoreType.DMA((6,)),
                 pltpu.SemaphoreType.DMA((4,)),
                 pltpu.SemaphoreType.DMA((2 * tiles,)),
@@ -419,6 +437,17 @@
                 collective_id=0, has_side_effects=True, vmem_limit_bytes=VMEM_BYTES
             ),
         )(slot_tile, tile_mask, token_count, queries, keys, values)
+        return pl.pallas_call(
+            settle,
+            out_shape=jax.ShapeDtypeStruct((tok, width), jnp.bfloat16),
+            in_specs=[pl.BlockSpec(memory_space=pl.ANY)],
+            out_specs=pl.BlockSpec(memory_space=pl.ANY),
+            scratch_shapes=[
+                pltpu.VMEM((tok, width), jnp.bfloat16),
+                pltpu.SemaphoreType.DMA((2, SETTLE_PARTS)),
+            ],
+            compiler_params=pltpu.CompilerParams(vmem_limit_bytes=VMEM_BYTES),
+        )(attended)
 
     return jax.shard_map(
         shards,

time: 195 us -> 194 us (level)
  local copies, waits for them, and re-layouts: 3.13 us -> 0 us
  Pallas kernels: 190 us -> 192 us
    unnamed x1 -> x0, local copies, waits for them, and re-layouts: 3.13 us -> none
    pallas_call x0 -> x1, Pallas kernels: none -> 2.42 us  [shards(): pl.pallas_call(settle, out_shape=jax.ShapeDtypeStruct((tok, width), jnp.b...]
where the time goes in v4:
time: 194 us; the launch traced here: 192 us
  Pallas kernels  192 us (99%)
    pallas_call x1, Pallas kernels, shards(): pl.pallas_call(functools.partial(kernel, slabs, tiles), out_shape=jax.Sha...  190 us

profile of v4, /device:TPU:27, one launch (start us, length us, event | category | flops | bytes accessed | tf_op | source)
XLA Modules:
  0.0 192.3 jit_solution(12100379451631503123)
XLA Ops:
  0.0 189.9 %shard_map.64.source = bf16[256,4096]{1,0:T(8,128)(2,1)} custom-call(s32[16,16]{1,0:T(8,128)} %slot_hbm.1, s32[16,16,48]{2,1,0:T(8,128)} %mask_hbm.1, s32[16,16]{1,0:T(8,128)} %count_hbm.1, bf16[256,4096]{1,0:T(8,128)(2,1)} %q_hbm.1, bf16[256,4096]{1,0:T(8,128)(2,1)} %k_hbm.1, bf16[256,4096]{1,0:T(8,128)(2,1)} %v_hbm.1), custom_call_target="tpu_custom_call" | custom-call | tf_op jit(solution)/shard_map/pallas_call | solution.py:399
  189.9 2.4 %shard_map.65 = bf16[256,4096]{1,0:T(8,128)(2,1)} custom-call(bf16[256,4096]{1,0:T(8,128)(2,1)} %shard_map.64.source), custom_call_target="tpu_custom_call" | custom-call | tf_op jit(solution)/shard_map/pallas_call | solution.py:440

commit v5 on v4

--- a/solution.py
+++ b/solution.py
@@ -97,14 +97,13 @@
         return {"tm": half * half_slabs + (place + half_slabs + way) % half_slabs}
 
     barrier = pltpu.get_barrier_semaphore()
-
-    def greet(step, carry):
-        pl.semaphore_signal(
-            barrier, inc=1, device_id=device(*partner(step)), device_id_type=MESH
-        )
-        return carry
-
-    lax.fori_loop(0, OWNERS - 1, greet, 0)
+    for reach in (4, 3, 5, 2, 6, 1, 7, 0):
+        for shift in range(SIDE):
+            if reach or shift:
+                other = (z + reach) % RING, (x + shift) % SIDE
+                pl.semaphore_signal(
+                    barrier, inc=1, device_id=device(*other), device_id_type=MESH
+                )
     for way in (1, -1):
         pl.semaphore_signal(barrier, inc=1, device_id=beside(way), device_id_type=MESH)
     for copy in first:

time: 194 us -> 194 us (level)
  no operation moved by 1% of the time
where the time goes in v5:
time: 194 us; the launch traced here: 192 us
  Pallas kernels  192 us (99%)
    pallas_call x1, Pallas kernels, shards(): pl.pallas_call(functools.partial(kernel, slabs, tiles), out_shape=jax.Sha...  190 us

profile of v5, /device:TPU:27, one launch (start us, length us, event | category | flops | bytes accessed | tf_op | source)
XLA Modules:
  0.0 192.2 jit_solution(14878671924310161041)
XLA Ops:
  0.0 189.7 %shard_map.64.source = bf16[256,4096]{1,0:T(8,128)(2,1)} custom-call(s32[16,16]{1,0:T(8,128)} %slot_hbm.1, s32[16,16,48]{2,1,0:T(8,128)} %mask_hbm.1, s32[16,16]{1,0:T(8,128)} %count_hbm.1, bf16[256,4096]{1,0:T(8,128)(2,1)} %q_hbm.1, bf16[256,4096]{1,0:T(8,128)(2,1)} %k_hbm.1, bf16[256,4096]{1,0:T(8,128)(2,1)} %v_hbm.1), custom_call_target="tpu_custom_call" | custom-call | tf_op jit(solution)/shard_map/pallas_call | solution.py:398
  189.7 2.4 %shard_map.65 = bf16[256,4096]{1,0:T(8,128)(2,1)} custom-call(bf16[256,4096]{1,0:T(8,128)(2,1)} %shard_map.64.source), custom_call_target="tpu_custom_call" | custom-call | tf_op jit(solution)/shard_map/pallas_call | solution.py:439

commit v6 on v5

--- a/solution.py
+++ b/solution.py
@@ -157,7 +157,11 @@
             ).start()
             return carry
 
-        lax.fori_loop(start, stop, send, 0)
+        if part == 0:
+            for step in range(start, stop):
+                send(step, 0)
+        else:
+            lax.fori_loop(start, stop, send, 0)
         if part == 1:
             keys[own_block] = k_block(head_columns(z, x))
         elif part == 3:

time: 194 us -> 194 us (level)
  no operation moved by 1% of the time
where the time goes in v6:
time: 194 us; the launch traced here: 192 us
  Pallas kernels  192 us (99%)
    pallas_call x1, Pallas kernels, shards(): pl.pallas_call(functools.partial(kernel, slabs, tiles), out_shape=jax.Sha...  190 us

profile of v6, /device:TPU:27, one launch (start us, length us, event | category | flops | bytes accessed | tf_op | source)
XLA Modules:
  0.0 192.1 jit_solution(1067873011031351498)
XLA Ops:
  0.0 189.7 %shard_map.64.source = bf16[256,4096]{1,0:T(8,128)(2,1)} custom-call(s32[16,16]{1,0:T(8,128)} %slot_hbm.1, s32[16,16,48]{2,1,0:T(8,128)} %mask_hbm.1, s32[16,16]{1,0:T(8,128)} %count_hbm.1, bf16[256,4096]{1,0:T(8,128)(2,1)} %q_hbm.1, bf16[256,4096]{1,0:T(8,128)(2,1)} %k_hbm.1, bf16[256,4096]{1,0:T(8,128)(2,1)} %v_hbm.1), custom_call_target="tpu_custom_call" | custom-call | tf_op jit(solution)/shard_map/pallas_call | solution.py:402
  189.7 2.4 %shard_map.65 = bf16[256,4096]{1,0:T(8,128)(2,1)} custom-call(bf16[256,4096]{1,0:T(8,128)(2,1)} %shard_map.64.source), custom_call_target="tpu_custom_call" | custom-call | tf_op jit(solution)/shard_map/pallas_call | solution.py:443
